TPU v7x, 128 devices: a whole 4x4x4 slice. The times are simulated.
128 devices in a mesh: dp: 32 (over x, y, core), mp: 2 (over z_lo), tower: 2 (over z_hi).
Axes of the slice: x: 4, y: 4, z: 4 (z_hi: 2, z_lo: 2; z = z_hi * 2 + z_lo), core: 2. Of those that a mesh axis runs over, the one named last changes fastest.
Arguments:
- features: bfloat16 [2, 16384, 1536], P('tower', 'dp'), may hold values from -16 to 16
- projection: bfloat16 [2, 1536, 1536], P('tower', None, 'mp'), may hold values from -1 to 1
- similarity_scale: float32 [1], replicated, may hold values from 8 to 16
- logit_bias: float32 [1], replicated, may hold values from -6 to -2
Outputs:
- row_loss: float32 [2, 16384], P('tower', ('dp', 'mp'))
- projection_grad: float32 [2, 1536, 1536], P('tower', None, 'mp')
All inputs are finite; a program needn't handle non-finite values.
Results may differ from a plain program's by a relative error of at most 0.00049.
Values may be sent and summed in bfloat16 or wider, within the bound.
No kernel may reach another device: no remote copies, remote signals or barrier semaphores. Data moves between devices by JAX's collectives and lax.ppermute only.
A program may use at most 192 MiB of HBM per device.

v0:
```python
import jax
import jax.numpy as jnp
from jax import lax
from jax.sharding import PartitionSpec as P


def swapped(block, axis, bit):
    count = lax.axis_size(axis)
    route = []
    for low in range(count):
        high = low | 1 << bit
        if high != low and high < count:
            route += [(low, high), (high, low)]
    return lax.ppermute(block, axis, route)


def pairwise_terms(
    self_rows, self_index, rows_per_block, portion_index, scale_factor, row_offset, batch_as_float
):
    pair_logits = (
        scale_factor
        * lax.dot_general(
            self_rows, rows_per_block, (((1,), (1,)), ((), ())), preferred_element_type=jnp.float32
        )
        + row_offset
    )
    labels = jnp.where(self_index[:, None] == portion_index[None, :], 1.0, -1.0).astype(jnp.float32)
    losses = jax.nn.softplus(-labels * pair_logits)
    pair_coefficient = (-labels * jax.nn.sigmoid(-labels * pair_logits) / batch_as_float).astype(
        jnp.bfloat16
    )
    loss_term = jnp.sum(losses, axis=1) / batch_as_float
    gradient_piece = scale_factor * jnp.dot(
        pair_coefficient, rows_per_block, preferred_element_type=jnp.float32
    )
    return (loss_term, gradient_piece)


def grad_of_proj(full_proj, inverse, grad_embed):
    along = jnp.sum(full_proj * grad_embed, axis=1, keepdims=True)
    cubed = inverse * inverse * inverse
    return inverse * grad_embed - cubed * full_proj * along


def on_device(features, projection, similarity_scale, logit_bias):
    rows_here = features.shape[1]
    groups = lax.axis_size("mp")
    share = rows_here // groups
    part_index = lax.axis_index("mp")
    batch_as_float = jnp.float32(rows_here * lax.axis_size("dp"))
    row_base = lax.axis_index("dp") * rows_here
    scale_factor = similarity_scale[0]
    row_offset = logit_bias[0]
    inputs = features[0]
    weight = projection[0]
    partial_proj = jnp.dot(inputs, weight, preferred_element_type=jnp.float32)
    full_proj = lax.all_gather(partial_proj, "mp", axis=1, tiled=True)
    inverse = lax.rsqrt(jnp.sum(full_proj * full_proj, axis=1, keepdims=True) + 1e-06)
    embedded = (full_proj * inverse).astype(jnp.bfloat16)
    partner_block = swapped(embedded, "tower", 0)
    self_rows = lax.dynamic_slice_in_dim(embedded, part_index * share, share, 0)
    self_index = row_base + part_index * share + jnp.arange(share, dtype=jnp.int32)
    rows_per_block = lax.all_gather(partner_block, "dp", axis=0, tiled=True)
    portion_index = jnp.arange(rows_per_block.shape[0], dtype=jnp.int32)
    loss_term, gradient_piece = pairwise_terms(
        self_rows,
        self_index,
        rows_per_block,
        portion_index,
        scale_factor,
        row_offset,
        batch_as_float,
    )
    proj_rows = lax.dynamic_slice_in_dim(full_proj, part_index * share, share, 0)
    inverse_rows = lax.dynamic_slice_in_dim(inverse, part_index * share, share, 0)
    grad_rows = grad_of_proj(proj_rows, inverse_rows, gradient_piece).astype(jnp.bfloat16)
    grad_cast = lax.all_to_all(grad_rows, "mp", split_axis=1, concat_axis=0, tiled=True)
    weight_part = lax.dot_general(
        inputs, grad_cast, (((0,), (0,)), ((), ())), preferred_element_type=jnp.float32
    )
    weight_grad = lax.psum(weight_part, "dp")
    return (loss_term[None], weight_grad[None])


def solution(mesh):
    placed = (P("tower", "dp", None), P("tower", None, "mp"), P(), P())
    return jax.shard_map(
        on_device,
        mesh=mesh,
        in_specs=placed,
        out_specs=(P("tower", ("dp", "mp")), P("tower", None, "mp")),
        check_vma=False,
    )
```

profile of v0, /device:TPU:1, one launch (start us, length us, event | category | flops | bytes accessed | tf_op | source)
XLA Modules:
  0.0 464.3 jit_solution(16976108732403815723)
XLA Ops:
  7.2 0.0 all-gather.3.cloned.1.call-start
  7.2 1.6 copy-done
  8.8 3.9 fusion.9
  12.8 0.0 all-gather.3.cloned.1.call-update
  12.8 0.0 all-gather.5.cloned.1.call-start
  12.8 50.8 %all-gather.3.cloned.1.call-done = f32[512,1536]{1,0:T(8,128)} async-done(((f32[512,768]{1,0:T(8,128)}), f32[512,1536]{1,0:T(8,128)}) %all-gather.3.cloned.1.call-update) | async-done | bytes 3145744 | tf_op jit(solution)/shard_map/all_gather | solution.py:57
  63.7 2.3 multiply_reduce_fusion
  66.0 0.5 copy-done.2
  66.5 1.4 multiply_convert_fusion.2
  67.9 2.6 collective-permute-start
  70.5 34.4 %collective-permute-done = bf16[512,1536]{1,0:T(8,128)(2,1)S(1)} collective-permute-done((bf16[512,1536]{1,0:T(8,128)(2,1)}, bf16[512,1536]{1,0:T(8,128)(2,1)S(1)}, u32[]{:S(2)}, u32[]{:S(2)}) %collective-permute-start) | collective-permute-done | bytes 1572896 | tf_op jit(solution)/shard_map/ppermute | solution.py:14
  104.9 1.1 copy-done.4
  106.0 0.0 all-reduce.2.cloned.1.call-start
  107.4 0.1 dynamic-slice.3
  107.5 158.3 %all-gather.5.cloned.1.call-done = bf16[16384,1536]{1,0:T(8,128)(2,1)} async-done(((bf16[512,1536]{1,0:T(8,128)(2,1)}), bf16[16384,1536]{1,0:T(8,128)(2,1)}) %all-gather.5.cloned.1.call-update) | async-done | bytes 50331664 | tf_op jit(solution)/shard_map/all_gather | solution.py:63
  265.8 28.6 %fusion.2 = (f32[256]{0:T(256)S(1)}, f32[256,16384]{1,0:T(8,128)}) fusion(f32[]{:T(128)} %bitcast.29, bf16[16384,1536]{1,0:T(8,128)(2,1)} %all-gather.5.cloned.1.call-done, bf16[512,1536]{1,0:T(8,128)(2,1)} %multiply_convert_fusion.2, s32[]{:T(128)S(6)} %select_n.14, f32[]{:T(128)} %bitcast.27, s32[256]{0:T(256)S(1)} %iota_add_fusion), kind=kOutput, calls=%fused_computation.4 | convolution fusion | flops 12939427840 | bytes 67898368 | tf_op jit(solution)/shard_map/dot_general | solution.py:22
  294.3 26.3 %multiply_reduce_fusion.1 = (f32[256]{0:T(256)S(1)}, f32[256,1536]{1,0:T(8,128)S(1)}) fusion(f32[512,1536]{1,0:T(8,128)} %all-gather.3.cloned.1.call-done, s32[]{:T(128)S(6)} %select_n.14, bf16[16384,1536]{1,0:T(8,128)(2,1)} %all-gather.5.cloned.1.call-done, f32[256,16384]{1,0:T(8,128)} %get-tuple-element.7, s32[256]{0:T(256)S(1)} %iota_add_fusion, f32[]{:T(128)} %bitcast.28), kind=kOutput, calls=%fused_computation.22 | convolution fusion | flops 12923830272 | bytes 70256648 | tf_op jit(solution)/shard_map/dot_general | solution.py:33
  320.6 1.8 subtract_convert_fusion
  322.5 0.1 copy.11
  322.6 12.8 %all_to_all.19 = bf16[256,2,768]{2,0,1:T(8,128)(2,1)S(1)} all-to-all(bf16[256,2,768]{2,0,1:T(8,128)(2,1)S(1)} %bitcast.31), channel_id=1, replica_groups=mesh['dp'=32,'mp'=2,'tower'=2] {'mp'}, dimensions={1} | all-to-all | bytes 1572864 | tf_op jit(solution)/shard_map/all_to_all | solution.py:77
  335.4 3.6 convolution_bitcast_fusion
  339.0 0.6 broadcast_multiply_fusion
  339.6 112.2 %all-reduce.2.cloned.1.call-done = f32[1,1536,768]{1,2,0:T(8,128)} async-done(((f32[1,1536,768]{1,2,0:T(8,128)}), f32[1,1536,768]{1,2,0:T(8,128)}) %all-reduce.2.cloned.1.call-update) | async-done | bytes 4718608 | tf_op jit(solution)/shard_map/psum | solution.py:81
  451.7 6.0 %copy.8 = f32[1,1536,768]{2,1,0:T(8,128)} copy(f32[1,1536,768]{1,2,0:T(8,128)} %all-reduce.2.cloned.1.call-done) | data formatting | bytes 9437184
  (12 shorter events, 0.1 us)
Async XLA Ops:
  7.2 1.7 copy-start
  7.2 56.5 %all-gather.3.cloned.1.call-start = ((), (), s32[]{:S(2)}) async-start(), calls=%async_computation.1 | async-start | bytes 4718592 | tf_op jit(solution)/shard_map/all_gather | solution.py:57
  12.8 253.0 %all-gather.5.cloned.1.call-start = ((), (), s32[]{:S(2)}) async-start(), calls=%async_computation.2 | async-start | bytes 51904512 | tf_op jit(solution)/shard_map/all_gather | solution.py:63
  63.7 2.8 copy-start.2
  67.9 37.0 %collective-permute-start = (bf16[512,1536]{1,0:T(8,128)(2,1)}, bf16[512,1536]{1,0:T(8,128)(2,1)S(1)}, u32[]{:S(2)}, u32[]{:S(2)}) collective-permute-start(bf16[512,1536]{1,0:T(8,128)(2,1)} %multiply_convert_fusion.2), channel_id=1, source_target_pairs={{0,1},{1,0},{2,3},{3,2},{4,5},{5,4},{6,7},{7,6},{8,9},{9,8},{10,11... | collective-permute-start | bytes 4718600 | tf_op jit(solution)/shard_map/ppermute | solution.py:14
  104.9 1.1 copy-start.4
  106.0 345.7 %all-reduce.2.cloned.1.call-start = ((), (), s32[]{:S(2)}) async-start(), calls=%async_computation.3 | async-start | bytes 9437184 | tf_op jit(solution)/shard_map/psum | solution.py:81
  320.6 14.7 %copy-start.3 = (bf16[1,512,1536]{2,1,0:T(8,128)(2,1)S(1)}, bf16[1,512,1536]{2,1,0:T(8,128)(2,1)}, u32[]{:S(2)}) copy-start(bf16[1,512,1536]{2,1,0:T(8,128)(2,1)} %param.4) | copy-start | bytes 4718596
  339.0 118.8 %copy-start.1 = (bf16[1,1536,768]{2,1,0:T(8,128)(2,1)S(1)}, bf16[1,1536,768]{2,1,0:T(8,128)(2,1)}, u32[]{:S(2)}) copy-start(bf16[1,1536,768]{2,1,0:T(8,128)(2,1)} %param.5) | copy-start | bytes 7077892
Sparse Core Ops, SparseCore 0:
  12.9 50.7 all-gather.2
  106.2 159.5 all-gather.4
  339.1 112.5 all-reduce.1
where the time goes:
time: 465 us; the launch traced here: 464 us
  waiting for transfers between devices  356 us (77%)
  matrix products  62.4 us (13%)
  between operations  15.1 us (3%)
  blocking collectives  12.8 us (3%)
  local copies, waits for them, and re-layouts  9.44 us (2%)
  other arithmetic  6.12 us (1%)
    all_gather x1, waiting for transfers between devices, on_device(): rows_per_block = lax.all_gather(partner_block, 'dp', axis=0, tiled=True)  158 us
    psum x1, waiting for transfers between devices, on_device(): weight_grad = lax.psum(weight_part, 'dp')  112 us
    all_gather x1, waiting for transfers between devices, on_device(): full_proj = lax.all_gather(partial_proj, 'mp', axis=1, tiled=True)  50.8 us
    ppermute x1, waiting for transfers between devices, swapped(): return lax.ppermute(block, axis, route)  34.4 us
    dot_general x1, matrix products, pairwise_terms(): lax.dot_general(self_rows, rows_per_block, (((1,), (1,)), ((), ())), pref...  28.6 us
    dot_general x1, matrix products, pairwise_terms(): jnp.dot(pair_coefficient, rows_per_block, preferred_element_type=jnp.floa...  26.3 us
    all_to_all x1, blocking collectives, on_device(): lax.all_to_all(grad_rows, 'mp', split_axis=1, concat_axis=0, tiled=True)  12.8 us
    unnamed x11, local copies, waits for them, and re-layouts  9.31 us
  transfers between devices with their start and end apart: 4, of which 4 were waited for; matrix products, arithmetic and copies ran while one was open for 0% of the time, Pallas kernels for 0%

commit v1 on v0

v1 whole, which is shorter than its diff:
```python
import functools

import jax
import jax.numpy as jnp
from jax import lax
from jax.experimental import pallas as pl
from jax.experimental.pallas import tpu as pltpu
from jax.sharding import Mesh, PartitionSpec as P

F32 = jnp.float32
BF16 = jnp.bfloat16
Z = ("m", "t")


def shifted(value, axes, step):
    count = lax.axis_size(axes)
    number = (lambda i: i % 2 * 2 + i // 2) if axes == Z else (lambda i: i)
    route = [(number(i), number((i + step) % count)) for i in range(count)]
    return lax.ppermute(value, axes, route)


def pick(block, index, size, axis=0):
    return lax.dynamic_slice_in_dim(block, index * size, size, axis)


def from_sources(own, send, axes, place):
    return [own] + [shifted(send((place + k) % 4), axes, k) for k in (2, 1, 3)]


ORDER = (0, 2, 1, 3)


def by_source(pieces, place):
    stacked = jnp.zeros((4,) + pieces[0].shape, pieces[0].dtype)
    for k, piece in zip(ORDER, pieces):
        stacked = lax.dynamic_update_index_in_dim(stacked, piece, (place - k) % 4, 0)
    return stacked


def tile_kernel(
    diag_ref, scale_ref, a_ref, b_ref, ga_ref, gb_ref, la_ref, lb_ref, acc_ref, loss_ref, c_ref
):
    step = pl.program_id(0)
    rows, width = a_ref.shape
    cols = b_ref.shape[0]
    sub = 256
    scale = scale_ref[0]
    bias = scale_ref[1]
    texts = b_ref[...]

    @pl.when(step == 0)
    def _():
        acc_ref[...] = jnp.zeros_like(acc_ref)
        loss_ref[...] = jnp.zeros_like(loss_ref)

    column_loss = jnp.zeros((1, cols), F32)
    for part in range(rows // sub):
        here = pl.ds(part * sub, sub)
        logits = (
            lax.dot_general(
                a_ref[here, :], texts, (((1,), (1,)), ((), ())), preferred_element_type=F32
            )
            * scale
            + bias
        )
        image = lax.broadcasted_iota(jnp.int32, (sub, cols), 0) + part * sub
        text = lax.broadcasted_iota(jnp.int32, (sub, cols), 1) + step * cols
        same = (text - image) == diag_ref[0]
        same = jnp.logical_and(same, (image // sub) == diag_ref[1])
        grown = jnp.exp(jnp.where(same, -logits, logits))
        whole = 1.0 + grown
        inverse = 1.0 / whole
        losses = jnp.log(whole) + (grown - (whole - 1.0)) * inverse
        share = grown * inverse
        c_ref[here, :] = jnp.where(same, -share, share).astype(BF16)
        loss_ref[here, :] += sum(
            losses[:, k * 128 : (k + 1) * 128] for k in range(cols // 128)
        )
        column_loss += jnp.sum(losses, axis=0, keepdims=True)
    lb_ref[0] = column_loss
    coefficient = c_ref[...]
    acc_ref[...] += jnp.dot(coefficient, texts, preferred_element_type=F32)
    gb_ref[...] = lax.dot_general(
        coefficient, a_ref[...], (((0,), (0,)), ((), ())), preferred_element_type=F32
    ).astype(gb_ref.dtype)

    @pl.when(step == pl.num_programs(0) - 1)
    def _():
        ga_ref[...] = acc_ref[...].astype(ga_ref.dtype)
        la_ref[...] = jnp.sum(loss_ref[...], axis=1, keepdims=True)


def tile_terms(images, texts, diag, scales):
    rows, width = images.shape
    count = texts.shape[0]
    cols = 512
    steps = count // cols
    smem = pl.BlockSpec(memory_space=pltpu.SMEM)
    return pl.pallas_call(
        tile_kernel,
        grid=(steps,),
        in_specs=[
            smem,
            smem,
            pl.BlockSpec((rows, width), lambda j: (0, 0)),
            pl.BlockSpec((cols, width), lambda j: (j, 0)),
        ],
        out_specs=[
            pl.BlockSpec((rows, width), lambda j: (0, 0)),
            pl.BlockSpec((cols, width), lambda j: (j, 0)),
            pl.BlockSpec((rows, 1), lambda j: (0, 0)),
            pl.BlockSpec((1, 1, cols), lambda j: (j, 0, 0)),
        ],
        out_shape=[
            jax.ShapeDtypeStruct((rows, width), BF16),
            jax.ShapeDtypeStruct((count, width), BF16),
            jax.ShapeDtypeStruct((rows, 1), F32),
            jax.ShapeDtypeStruct((steps, 1, cols), F32),
        ],
        scratch_shapes=[
            pltpu.VMEM((rows, width), F32),
            pltpu.VMEM((rows, 128), F32),
            pltpu.VMEM((rows, cols), BF16),
        ],
        compiler_params=pltpu.CompilerParams(vmem_limit_bytes=56 * 2**20),
        cost_estimate=pl.CostEstimate(
            flops=6 * rows * count * width,
            bytes_accessed=4 * (rows + count) * width,
            transcendentals=3 * rows * count,
        ),
    )(diag, scales, images, texts)


def summed_piece(blocks, axis, place):
    pieces = from_sources(
        lax.dynamic_index_in_dim(blocks, place, 0, False),
        lambda d: lax.dynamic_index_in_dim(blocks, d, 0, False),
        axis,
        place,
    )
    return sum(piece.astype(F32) for piece in pieces)


def gathered(block, axis, place):
    return by_source(from_sources(block, lambda d: block, axis, place), place)


def on_device(features, projection, similarity_scale, logit_bias):
    x, y, c = lax.axis_index("x"), lax.axis_index("y"), lax.axis_index("c")
    m, t = lax.axis_index("m"), lax.axis_index("t")
    z = t * 2 + m
    inputs = features[0]
    rows, width = inputs.shape
    weight = projection[0]
    half = weight.shape[1]
    part = rows // 2
    pairs = rows * 32
    scale_factor = similarity_scale[0]

    projected = jnp.dot(inputs, weight, preferred_element_type=F32)
    squares = lax.psum(jnp.sum(projected * projected, axis=1), "m")[:, None]
    inverse = lax.rsqrt(squares + 1e-06)
    embedded = (projected * inverse).astype(BF16)
    mine = pick(inputs, c, half, 1)
    others = shifted(pick(inputs, 1 - c, half, 1), "c", 1)

    def rows_for(d):
        return pick(embedded, jnp.where(t == 0, d % 2, d // 2), part)

    arrived = by_source(from_sources(rows_for(z), rows_for, Z, z), z)
    image = jnp.concatenate([arrived[0], arrived[1]], axis=1)
    text = jnp.concatenate([arrived[2], arrived[3]], axis=1)

    images = gathered(image, "y", y).reshape(4 * part, width)
    texts_core = gathered(text, "x", x)
    texts_other = shifted(texts_core, "c", 1)
    first = jnp.where(c == 0, texts_core, texts_other)
    second = jnp.where(c == 0, texts_other, texts_core)
    texts = jnp.stack([first, second]).reshape(8 * part, width)

    offset = ((c * 4 + x) - y) * part
    diag = jnp.stack([offset, jnp.where(m == t, y, -1)]).astype(jnp.int32)
    scales = jnp.stack([scale_factor, logit_bias[0]])
    grad_a, grad_b, loss_a, loss_b = tile_terms(images, texts, diag, scales)

    grad_a = summed_piece(grad_a.reshape(4, part, width), "y", y)
    grad_b = grad_b.reshape(2, 4, part, width)
    kept = lax.dynamic_index_in_dim(grad_b, c, 0, False)
    given = shifted(lax.dynamic_index_in_dim(grad_b, 1 - c, 0, False), "c", 1)
    grad_b = summed_piece((kept.astype(F32) + given.astype(F32)).astype(BF16), "x", x)

    both = jnp.stack([grad_a, grad_b]).astype(BF16)

    def columns_for(d):
        return pick(lax.dynamic_index_in_dim(both, d // 2, 0, False), d % 2, half, 1)

    arrived = by_source(from_sources(columns_for(z), columns_for, Z, z), z).astype(F32)
    from_image = jnp.stack([arrived[0] + arrived[2], arrived[1] + arrived[3]])
    from_text = jnp.stack([arrived[0] + arrived[1], arrived[2] + arrived[3]])
    grad_embed = jnp.where(t == 0, from_image, from_text).reshape(rows, half)
    grad_embed = grad_embed * (scale_factor / pairs)

    along = lax.psum(jnp.sum(projected * grad_embed, axis=1), "m")[:, None]
    cubed = inverse * inverse * inverse
    grad_proj = (inverse * grad_embed - cubed * projected * along).astype(BF16)
    grad_other = shifted(grad_proj, "c", 1)
    weight_part = lax.dot_general(
        mine, grad_proj, (((0,), (0,)), ((), ())), preferred_element_type=F32
    ) + lax.dot_general(others, grad_other, (((0,), (0,)), ((), ())), preferred_element_type=F32)

    quarter = half // 2
    one = summed_piece(weight_part[:quarter].reshape(4, quarter // 4, half), "x", x)
    two = summed_piece(weight_part[quarter:].reshape(4, quarter // 4, half), "y", y)
    one = sum(from_sources(one, lambda d: one, "y", y))
    two = sum(from_sources(two, lambda d: two, "x", x))
    one = gathered(one, "x", x).reshape(quarter, half)
    two = gathered(two, "y", y).reshape(quarter, half)
    whole = jnp.concatenate([one, two], axis=0)
    swapped = shifted(whole, "c", 1)
    weight_grad = jnp.concatenate(
        [jnp.where(c == 0, whole, swapped), jnp.where(c == 0, swapped, whole)], axis=0
    )

    loss_a = summed_piece(loss_a.reshape(4, part), "y", y)
    loss_a = loss_a + shifted(loss_a, "t", 1)
    loss_b = loss_b.reshape(2, 4, part)
    loss_b = lax.dynamic_index_in_dim(loss_b, c, 0, False) + shifted(
        lax.dynamic_index_in_dim(loss_b, 1 - c, 0, False), "c", 1
    )
    loss_b = summed_piece(loss_b, "x", x)
    loss_b = loss_b + shifted(loss_b, "m", 1)
    loss_b = jnp.where(t == m, loss_b, shifted(loss_b, "t", 1))
    row_loss = jnp.where(t == 0, loss_a, loss_b) / pairs
    return (row_loss[None], weight_grad[None])


def solution(mesh):
    fine = Mesh(mesh.devices.reshape(4, 4, 2, 2, 2), ("x", "y", "c", "m", "t"))
    dp = ("x", "y", "c")
    placed = (P("t", dp, None), P("t", None, "m"), P(), P())
    return jax.shard_map(
        on_device,
        mesh=fine,
        in_specs=placed,
        out_specs=(P("t", dp + ("m",)), P("t", None, "m")),
        check_vma=False,
    )
```

time: 465 us -> 338 us (0.73)
  the two profiles are of different devices: /device:TPU:1 before, /device:TPU:0 now
where the time goes in v1:
time: 338 us; the launch traced here: 332 us
  waiting for transfers between devices  154 us (46%)
  starting transfers between devices  72.4 us (21%)
  other arithmetic  30.6 us (9%)
  Pallas kernels  30.5 us (9%)
  local copies, waits for them, and re-layouts  24.3 us (7%)
  blocking collectives  9.86 us (3%)
  matrix products  8.14 us (2%)
    ppermute x51, waiting for transfers between devices, shifted(): return lax.ppermute(value, axes, route)  154 us
    ppermute x51, starting transfers between devices, shifted(): return lax.ppermute(value, axes, route)  72.4 us
    pallas_call x1, Pallas kernels, tile_terms(): pl.pallas_call(tile_kernel, grid=(steps,), in_specs=[smem, smem, pl.Block...  30.5 us
    another operation x2, other arithmetic, on_device(): texts = jnp.stack([first, second]).reshape(8 * part, width)  7.61 us
    dynamic_update_slice x19, local copies, waits for them, and re-layouts, by_source(): lax.dynamic_update_index_in_dim(stacked, piece, (place - k) % 4, 0)  7.51 us
  transfers between devices with their start and end apart: 51, of which 25 were waited for; matrix products, arithmetic and copies ran while one was open for 8% of the time, Pallas kernels for 0%

profile of v1, /device:TPU:0, one launch (start us, length us, event | category | flops | bytes accessed | tf_op | source)
XLA Modules:
  0.0 332.4 jit_solution(18157124525531428872)
XLA Ops:
  2.3 4.0 %multiply_reduce_fusion = (f32[512]{0:T(512)S(1)}, f32[512,768]{1,0:T(8,128)}) fusion(bf16[1,1536,768]{2,1,0:T(8,128)(2,1)S(1)} %copy-done, bf16[1,512,1536]{2,1,0:T(8,128)(2,1)} %param.4), kind=kOutput, calls=%fused_computation.36 | convolution fusion | flops 1208745472 | bytes 5507072 | tf_op jit(solution)/shard_map/dot_general | solution.py:160
  6.3 4.9 %psum.14 = f32[512]{0:T(512)S(1)} all-reduce(f32[512]{0:T(512)S(1)} %get-tuple-element.57), channel_id=1, replica_groups=mesh['x'=4,'y'=4,'c'=2,'m'=2,'t'=2] {'m'}, use_global_device_ids=true, to_apply=%region_1.0 | all-reduce | flops 512 | bytes 4096 | tf_op jit(solution)/shard_map/psum | solution.py:161
  12.9 4.0 %collective-permute-start = (bf16[256,768]{1,0:T(8,128)(2,1)S(1)}, bf16[256,768]{1,0:T(8,128)(2,1)}, u32[]{:S(2)}, u32[]{:S(2)}) collective-permute-start(bf16[256,768]{1,0:T(8,128)(2,1)S(1)} %get-tuple-element.46), channel_id=1, source_target_pairs={{0,1},{2,3},{1,0},{3,2},{4,5},{6,7},{5,4},{7,6},{8,9},{10,11},{9,8... | collective-permute-start | bytes 1179656 | tf_op jit(solution)/shard_map/ppermute | solution.py:19
  20.3 6.8 %collective-permute-done = bf16[256,768]{1,0:T(8,128)(2,1)} collective-permute-done((bf16[256,768]{1,0:T(8,128)(2,1)S(1)}, bf16[256,768]{1,0:T(8,128)(2,1)}, u32[]{:S(2)}, u32[]{:S(2)}) %collective-permute-start) | collective-permute-done | bytes 393248 | tf_op jit(solution)/shard_map/ppermute | solution.py:19
  28.1 5.3 %collective-permute-done.1 = bf16[256,768]{1,0:T(8,128)(2,1)} collective-permute-done((bf16[256,768]{1,0:T(8,128)(2,1)S(1)}, bf16[256,768]{1,0:T(8,128)(2,1)}, u32[]{:S(2)}, u32[]{:S(2)}) %collective-permute-start.1) | collective-permute-done | bytes 393248 | tf_op jit(solution)/shard_map/ppermute | solution.py:19
  44.8 12.9 %collective-permute-done.6 = bf16[256,1536]{1,0:T(8,128)(2,1)} collective-permute-done((bf16[256,1536]{1,0:T(8,128)(2,1)S(1)}, bf16[256,1536]{1,0:T(8,128)(2,1)}, u32[]{:S(2)}, u32[]{:S(2)}) %collective-permute-start.6) | collective-permute-done | bytes 786464 | tf_op jit(solution)/shard_map/ppermute | solution.py:19
  59.9 13.7 %collective-permute-done.7 = bf16[256,1536]{1,0:T(8,128)(2,1)S(1)} collective-permute-done((bf16[256,1536]{1,0:T(8,128)(2,1)S(1)}, bf16[256,1536]{1,0:T(8,128)(2,1)S(1)}, u32[]{:S(2)}, u32[]{:S(2)}) %collective-permute-start.7) | collective-permute-done | bytes 786464 | tf_op jit(solution)/shard_map/ppermute | solution.py:19
  85.0 12.5 %collective-permute-done.3 = bf16[256,1536]{1,0:T(8,128)(2,1)S(1)} collective-permute-done((bf16[256,1536]{1,0:T(8,128)(2,1)S(1)}, bf16[256,1536]{1,0:T(8,128)(2,1)S(1)}, u32[]{:S(2)}, u32[]{:S(2)}) %collective-permute-start.3) | collective-permute-done | bytes 786464 | tf_op jit(solution)/shard_map/ppermute | solution.py:19
  97.6 16.4 %collective-permute-done.4 = bf16[256,1536]{1,0:T(8,128)(2,1)S(1)} collective-permute-done((bf16[256,1536]{1,0:T(8,128)(2,1)S(1)}, bf16[256,1536]{1,0:T(8,128)(2,1)S(1)}, u32[]{:S(2)}, u32[]{:S(2)}) %collective-permute-start.4) | collective-permute-done | bytes 786464 | tf_op jit(solution)/shard_map/ppermute | solution.py:19
  114.4 4.4 %select_bitcast_fusion.1 = (bf16[1,4,256,1536]{3,2,1,0:T(8,128)(2,1)S(1)}, bf16[1,4,256,1536]{3,2,1,0:T(8,128)(2,1)S(1)}) fusion(bf16[4,256,1536]{2,1,0:T(8,128)(2,1)} %bitcast_dynamic-update-slice_fusion, bf16[4,256,1536]{2,1,0:T(8,128)(2,1)} %collective-permute-done.9, pred[]{:T(512)S(6)} %eq.79), kind=kLoop, calls=%fused_computation.6 | loop fusion | flops 3145728 | bytes 12582913 | tf_op jit(solution)/shard_map/stack | solution.py:179
  122.0 30.5 %shard_map.59 = (bf16[1024,1536]{1,0:T(8,128)(2,1)}, bf16[2048,1536]{1,0:T(8,128)(2,1)}, f32[1024,1]{1,0:T(8,128)}, f32[4,1,512]{2,1,0:T(1,128)}) custom-call(s32[2]{0:T(128)} %pad_add_fusion.diag_ref, f32[2]{0:T(128)} %pad_maximum_fusion.4.scale_ref, bf16[1024,1536]{1,0:T(8,128)(2,1)} %bitcast.181, bf16[2048,1536]{1,0:T(8,128)(2,1)} %bitcast.174), custom_call_target="tpu_custom_call" | custom-call | flops 19327352832 | bytes 18874368 | tf_op jit(solution)/shard_map/pallas_call | solution.py:99
  152.5 3.8 %dynamic-slice_bitcast_fusion = bf16[4,256,1536]{2,1,0:T(8,128)(2,1)} fusion(bf16[2,4,256,1536]{3,2,1,0:T(8,128)(2,1)} %bitcast.175, s32[]{:T(128)S(6)} %select_n.466), kind=kLoop, calls=%fused_computation.4 | loop fusion | bytes 6291460 | tf_op jit(solution)/shard_map/jit(dynamic_index_in_dim)/squeeze | solution.py:189
  173.9 6.9 %collective-permute-done.20 = bf16[256,1536]{1,0:T(8,128)(2,1)S(1)} collective-permute-done((bf16[256,1536]{1,0:T(8,128)(2,1)S(1)}, bf16[256,1536]{1,0:T(8,128)(2,1)S(1)}, u32[]{:S(2)}, u32[]{:S(2)}) %collective-permute-start.20) | collective-permute-done | bytes 786464 | tf_op jit(solution)/shard_map/ppermute | solution.py:19
  182.7 14.5 %collective-permute-done.21 = bf16[256,1536]{1,0:T(8,128)(2,1)S(1)} collective-permute-done((bf16[256,1536]{1,0:T(8,128)(2,1)}, bf16[256,1536]{1,0:T(8,128)(2,1)S(1)}, u32[]{:S(2)}, u32[]{:S(2)}) %collective-permute-start.21) | collective-permute-done | bytes 786464 | tf_op jit(solution)/shard_map/ppermute | solution.py:19
  198.7 10.2 %collective-permute-done.25 = bf16[256,1536]{1,0:T(8,128)(2,1)} collective-permute-done((bf16[256,1536]{1,0:T(8,128)(2,1)}, bf16[256,1536]{1,0:T(8,128)(2,1)}, u32[]{:S(2)}, u32[]{:S(2)}) %collective-permute-start.25) | collective-permute-done | bytes 786464 | tf_op jit(solution)/shard_map/ppermute | solution.py:19
  220.5 5.9 %collective-permute-done.27 = bf16[256,768]{1,0:T(8,128)(2,1)S(1)} collective-permute-done((bf16[256,768]{1,0:T(8,128)(2,1)S(1)}, bf16[256,768]{1,0:T(8,128)(2,1)S(1)}, u32[]{:S(2)}, u32[]{:S(2)}) %collective-permute-start.27) | collective-permute-done | bytes 393248 | tf_op jit(solution)/shard_map/ppermute | solution.py:19
  226.5 7.4 %collective-permute-done.28 = bf16[256,768]{1,0:T(8,128)(2,1)S(1)} collective-permute-done((bf16[256,768]{1,0:T(8,128)(2,1)S(1)}, bf16[256,768]{1,0:T(8,128)(2,1)S(1)}, u32[]{:S(2)}, u32[]{:S(2)}) %collective-permute-start.28) | collective-permute-done | bytes 393248 | tf_op jit(solution)/shard_map/ppermute | solution.py:19
  236.3 4.9 %psum.15 = f32[512]{0:T(512)S(1)} all-reduce(f32[512]{0:T(512)S(1)} %fusion.12), channel_id=1, replica_groups=mesh['x'=4,'y'=4,'c'=2,'m'=2,'t'=2] {'m'}, use_global_device_ids=true, to_apply=%region_3.4 | all-reduce | flops 512 | bytes 4096 | tf_op jit(solution)/shard_map/psum | solution.py:203
  254.0 5.6 %collective-permute-done.32 = f32[96,768]{1,0:T(8,128)S(1)} collective-permute-done((f32[96,768]{1,0:T(8,128)S(1)}, f32[96,768]{1,0:T(8,128)S(1)}, u32[]{:S(2)}, u32[]{:S(2)}) %collective-permute-start.32) | collective-permute-done | bytes 294944 | tf_op jit(solution)/shard_map/ppermute | solution.py:19
  259.8 5.2 %collective-permute-done.33 = f32[96,768]{1,0:T(8,128)S(1)} collective-permute-done((f32[96,768]{1,0:T(8,128)S(1)}, f32[96,768]{1,0:T(8,128)S(1)}, u32[]{:S(2)}, u32[]{:S(2)}) %collective-permute-start.33) | collective-permute-done | bytes 294944 | tf_op jit(solution)/shard_map/ppermute | solution.py:19
  271.7 4.8 %collective-permute-done.35 = f32[96,768]{1,0:T(8,128)S(1)} collective-permute-done((f32[96,768]{1,0:T(8,128)S(1)}, f32[96,768]{1,0:T(8,128)S(1)}, u32[]{:S(2)}, u32[]{:S(2)}) %collective-permute-start.35) | collective-permute-done | bytes 294944 | tf_op jit(solution)/shard_map/ppermute | solution.py:19
  288.8 5.0 %collective-permute-done.38 = f32[96,768]{1,0:T(8,128)S(1)} collective-permute-done((f32[96,768]{1,0:T(8,128)S(1)}, f32[96,768]{1,0:T(8,128)S(1)}, u32[]{:S(2)}, u32[]{:S(2)}) %collective-permute-start.38) | collective-permute-done | bytes 294944 | tf_op jit(solution)/shard_map/ppermute | solution.py:19
  294.5 4.7 %collective-permute-done.39 = f32[96,768]{1,0:T(8,128)S(1)} collective-permute-done((f32[96,768]{1,0:T(8,128)S(1)}, f32[96,768]{1,0:T(8,128)S(1)}, u32[]{:S(2)}, u32[]{:S(2)}) %collective-permute-start.39) | collective-permute-done | bytes 294944 | tf_op jit(solution)/shard_map/ppermute | solution.py:19
  299.3 4.0 %collective-permute-done.48 = f32[96,768]{1,0:T(8,128)S(1)} collective-permute-done((f32[96,768]{1,0:T(8,128)S(1)}, f32[96,768]{1,0:T(8,128)S(1)}, u32[]{:S(2)}, u32[]{:S(2)}) %collective-permute-start.48) | collective-permute-done | bytes 294944 | tf_op jit(solution)/shard_map/ppermute | solution.py:19
  (170 shorter events, 131.2 us)
Async XLA Ops:
  16.9 16.5 %collective-permute-start.1 = (bf16[256,768]{1,0:T(8,128)(2,1)S(1)}, bf16[256,768]{1,0:T(8,128)(2,1)}, u32[]{:S(2)}, u32[]{:S(2)}) collective-permute-start(bf16[256,768]{1,0:T(8,128)(2,1)S(1)} %get-tuple-element.45), channel_id=1, source_target_pairs={{0,2},{2,1},{1,3},{3,0},{4,6},{6,5},{5,7},{7,4},{8,10},{10,9},{9,1... | collective-permute-start | bytes 1179656 | tf_op jit(solution)/shard_map/ppermute | solution.py:19
  17.9 16.5 %collective-permute-start.2 = (bf16[256,768]{1,0:T(8,128)(2,1)S(1)}, bf16[256,768]{1,0:T(8,128)(2,1)}, u32[]{:S(2)}, u32[]{:S(2)}) collective-permute-start(bf16[256,768]{1,0:T(8,128)(2,1)S(1)} %get-tuple-element.44), channel_id=1, source_target_pairs={{0,3},{2,0},{1,2},{3,1},{4,7},{6,4},{5,6},{7,5},{8,11},{10,8},{9,1... | collective-permute-start | bytes 1179656 | tf_op jit(solution)/shard_map/ppermute | solution.py:19
  35.6 22.1 %collective-permute-start.6 = (bf16[256,1536]{1,0:T(8,128)(2,1)S(1)}, bf16[256,1536]{1,0:T(8,128)(2,1)}, u32[]{:S(2)}, u32[]{:S(2)}) collective-permute-start(bf16[256,1536]{1,0:T(8,128)(2,1)S(1)} %pad_maximum_fusion.3), channel_id=1, source_target_pairs={{0,64},{32,96},{64,0},{96,32},{1,65},{33,97},{65,1},{97,33},{2,66}... | collective-permute-start | bytes 2359304 | tf_op jit(solution)/shard_map/ppermute | solution.py:19
  38.8 34.8 %collective-permute-start.7 = (bf16[256,1536]{1,0:T(8,128)(2,1)S(1)}, bf16[256,1536]{1,0:T(8,128)(2,1)S(1)}, u32[]{:S(2)}, u32[]{:S(2)}) collective-permute-start(bf16[256,1536]{1,0:T(8,128)(2,1)S(1)} %pad_maximum_fusion.3), channel_id=1, source_target_pairs={{0,32},{32,64},{64,96},{96,0},{1,33},{33,65},{65,97},{97,1},{2,34}... | collective-permute-start | bytes 2359304 | tf_op jit(solution)/shard_map/ppermute | solution.py:19
  39.3 35.2 %collective-permute-start.8 = (bf16[256,1536]{1,0:T(8,128)(2,1)S(1)}, bf16[256,1536]{1,0:T(8,128)(2,1)S(1)}, u32[]{:S(2)}, u32[]{:S(2)}) collective-permute-start(bf16[256,1536]{1,0:T(8,128)(2,1)S(1)} %pad_maximum_fusion.3), channel_id=1, source_target_pairs={{0,96},{32,0},{64,32},{96,64},{1,97},{33,1},{65,33},{97,65},{2,98}... | collective-permute-start | bytes 2359304 | tf_op jit(solution)/shard_map/ppermute | solution.py:19
  75.5 38.9 %collective-permute-start.9 = (bf16[4,256,1536]{2,1,0:T(8,128)(2,1)}, bf16[4,256,1536]{2,1,0:T(8,128)(2,1)}, u32[]{:S(2)}, u32[]{:S(2)}) collective-permute-start(bf16[4,256,1536]{2,1,0:T(8,128)(2,1)} %bitcast_dynamic-update-slice_fusion), channel_id=1, source_target_pairs={{0,4},{4,0},{1,5},{5,1},{2,6},{6,2},{3,7},{7,3},{8,12},{12,8},{9,1... | collective-permute-start | bytes 9437192 | tf_op jit(solution)/shard_map/ppermute | solution.py:19
  75.5 22.0 %collective-permute-start.3 = (bf16[256,1536]{1,0:T(8,128)(2,1)S(1)}, bf16[256,1536]{1,0:T(8,128)(2,1)S(1)}, u32[]{:S(2)}, u32[]{:S(2)}) collective-permute-start(bf16[256,1536]{1,0:T(8,128)(2,1)S(1)} %pad_maximum_fusion.2), channel_id=1, source_target_pairs={{0,16},{8,24},{16,0},{24,8},{1,17},{9,25},{17,1},{25,9},{2,18},{10... | collective-permute-start | bytes 2359304 | tf_op jit(solution)/shard_map/ppermute | solution.py:19
  80.7 33.2 %collective-permute-start.4 = (bf16[256,1536]{1,0:T(8,128)(2,1)S(1)}, bf16[256,1536]{1,0:T(8,128)(2,1)S(1)}, u32[]{:S(2)}, u32[]{:S(2)}) collective-permute-start(bf16[256,1536]{1,0:T(8,128)(2,1)S(1)} %pad_maximum_fusion.2), channel_id=1, source_target_pairs={{0,8},{8,16},{16,24},{24,0},{1,9},{9,17},{17,25},{25,1},{2,10},{10... | collective-permute-start | bytes 2359304 | tf_op jit(solution)/shard_map/ppermute | solution.py:19
  81.9 32.4 %collective-permute-start.5 = (bf16[256,1536]{1,0:T(8,128)(2,1)S(1)}, bf16[256,1536]{1,0:T(8,128)(2,1)S(1)}, u32[]{:S(2)}, u32[]{:S(2)}) collective-permute-start(bf16[256,1536]{1,0:T(8,128)(2,1)S(1)} %pad_maximum_fusion.2), channel_id=1, source_target_pairs={{0,24},{8,0},{16,8},{24,16},{1,25},{9,1},{17,9},{25,17},{2,26},{10... | collective-permute-start | bytes 2359304 | tf_op jit(solution)/shard_map/ppermute | solution.py:19
  158.9 21.9 %collective-permute-start.20 = (bf16[256,1536]{1,0:T(8,128)(2,1)S(1)}, bf16[256,1536]{1,0:T(8,128)(2,1)S(1)}, u32[]{:S(2)}, u32[]{:S(2)}) collective-permute-start(bf16[256,1536]{1,0:T(8,128)(2,1)S(1)} %get-tuple-element.25), channel_id=1, source_target_pairs={{0,16},{8,24},{16,0},{24,8},{1,17},{9,25},{17,1},{25,9},{2,18},{10... | collective-permute-start | bytes 2359304 | tf_op jit(solution)/shard_map/ppermute | solution.py:19
  161.8 35.4 %collective-permute-start.21 = (bf16[256,1536]{1,0:T(8,128)(2,1)}, bf16[256,1536]{1,0:T(8,128)(2,1)S(1)}, u32[]{:S(2)}, u32[]{:S(2)}) collective-permute-start(bf16[256,1536]{1,0:T(8,128)(2,1)} %get-tuple-element.27), channel_id=1, source_target_pairs={{0,8},{8,16},{16,24},{24,0},{1,9},{9,17},{17,25},{25,1},{2,10},{10... | collective-permute-start | bytes 2359304 | tf_op jit(solution)/shard_map/ppermute | solution.py:19
  162.4 34.8 %collective-permute-start.22 = (bf16[256,1536]{1,0:T(8,128)(2,1)S(1)}, bf16[256,1536]{1,0:T(8,128)(2,1)S(1)}, u32[]{:S(2)}, u32[]{:S(2)}) collective-permute-start(bf16[256,1536]{1,0:T(8,128)(2,1)S(1)} %get-tuple-element.26), channel_id=1, source_target_pairs={{0,24},{8,0},{16,8},{24,16},{1,25},{9,1},{17,9},{25,17},{2,26},{10... | collective-permute-start | bytes 2359304 | tf_op jit(solution)/shard_map/ppermute | solution.py:19
  171.2 27.5 %collective-permute-start.24 = (bf16[256,1536]{1,0:T(8,128)(2,1)}, bf16[256,1536]{1,0:T(8,128)(2,1)}, u32[]{:S(2)}, u32[]{:S(2)}) collective-permute-start(bf16[256,1536]{1,0:T(8,128)(2,1)} %get-tuple-element.22), channel_id=1, source_target_pairs={{0,64},{32,96},{64,0},{96,32},{1,65},{33,97},{65,1},{97,33},{2,66}... | collective-permute-start | bytes 2359304 | tf_op jit(solution)/shard_map/ppermute | solution.py:19
  173.4 35.6 %collective-permute-start.25 = (bf16[256,1536]{1,0:T(8,128)(2,1)}, bf16[256,1536]{1,0:T(8,128)(2,1)}, u32[]{:S(2)}, u32[]{:S(2)}) collective-permute-start(bf16[256,1536]{1,0:T(8,128)(2,1)} %get-tuple-element.24), channel_id=1, source_target_pairs={{0,32},{32,64},{64,96},{96,0},{1,33},{33,65},{65,97},{97,1},{2,34}... | collective-permute-start | bytes 2359304 | tf_op jit(solution)/shard_map/ppermute | solution.py:19
  180.8 28.2 %collective-permute-start.26 = (bf16[256,1536]{1,0:T(8,128)(2,1)}, bf16[256,1536]{1,0:T(8,128)(2,1)}, u32[]{:S(2)}, u32[]{:S(2)}) collective-permute-start(bf16[256,1536]{1,0:T(8,128)(2,1)} %get-tuple-element.23), channel_id=1, source_target_pairs={{0,96},{32,0},{64,32},{96,64},{1,97},{33,1},{65,33},{97,65},{2,98}... | collective-permute-start | bytes 2359304 | tf_op jit(solution)/shard_map/ppermute | solution.py:19
  215.2 18.7 %collective-permute-start.28 = (bf16[256,768]{1,0:T(8,128)(2,1)S(1)}, bf16[256,768]{1,0:T(8,128)(2,1)S(1)}, u32[]{:S(2)}, u32[]{:S(2)}) collective-permute-start(bf16[256,768]{1,0:T(8,128)(2,1)S(1)} %get-tuple-element.33), channel_id=1, source_target_pairs={{0,2},{2,1},{1,3},{3,0},{4,6},{6,5},{5,7},{7,4},{8,10},{10,9},{9,1... | collective-permute-start | bytes 1179656 | tf_op jit(solution)/shard_map/ppermute | solution.py:19
  218.2 26.9 %collective-permute-start.30 = (bf16[512,768]{1,0:T(8,128)(2,1)}, bf16[512,768]{1,0:T(8,128)(2,1)}, u32[]{:S(2)}, u32[]{:S(2)}) collective-permute-start(bf16[512,768]{1,0:T(8,128)(2,1)} %dynamic-slice_bitcast_fusion.1), channel_id=1, source_target_pairs={{0,4},{4,0},{1,5},{5,1},{2,6},{6,2},{3,7},{7,3},{8,12},{12,8},{9,1... | collective-permute-start | bytes 2359304 | tf_op jit(solution)/shard_map/ppermute | solution.py:19
  218.2 15.7 %collective-permute-start.29 = (bf16[256,768]{1,0:T(8,128)(2,1)S(1)}, bf16[256,768]{1,0:T(8,128)(2,1)S(1)}, u32[]{:S(2)}, u32[]{:S(2)}) collective-permute-start(bf16[256,768]{1,0:T(8,128)(2,1)S(1)} %get-tuple-element.30), channel_id=1, source_target_pairs={{0,3},{2,0},{1,2},{3,1},{4,7},{6,4},{5,6},{7,5},{8,11},{10,8},{9,1... | collective-permute-start | bytes 1179656 | tf_op jit(solution)/shard_map/ppermute | solution.py:19
  249.4 15.6 %collective-permute-start.33 = (f32[96,768]{1,0:T(8,128)S(1)}, f32[96,768]{1,0:T(8,128)S(1)}, u32[]{:S(2)}, u32[]{:S(2)}) collective-permute-start(f32[96,768]{1,0:T(8,128)S(1)} %get-tuple-element.40), channel_id=1, source_target_pairs={{0,32},{32,64},{64,96},{96,0},{1,33},{33,65},{65,97},{97,1},{2,34}... | collective-permute-start | bytes 884744 | tf_op jit(solution)/shard_map/ppermute | solution.py:19
  265.7 16.2 %collective-permute-start.36 = (f32[96,768]{1,0:T(8,128)S(1)}, f32[96,768]{1,0:T(8,128)S(1)}, u32[]{:S(2)}, u32[]{:S(2)}) collective-permute-start(f32[96,768]{1,0:T(8,128)S(1)} %fusion.30), channel_id=1, source_target_pairs={{0,8},{8,16},{16,24},{24,0},{1,9},{9,17},{17,25},{25,1},{2,10},{10... | collective-permute-start | bytes 884744 | tf_op jit(solution)/shard_map/ppermute | solution.py:19
  266.3 15.6 %collective-permute-start.37 = (f32[96,768]{1,0:T(8,128)S(1)}, f32[96,768]{1,0:T(8,128)S(1)}, u32[]{:S(2)}, u32[]{:S(2)}) collective-permute-start(f32[96,768]{1,0:T(8,128)S(1)} %fusion.30), channel_id=1, source_target_pairs={{0,24},{8,0},{16,8},{24,16},{1,25},{9,1},{17,9},{25,17},{2,26},{10... | collective-permute-start | bytes 884744 | tf_op jit(solution)/shard_map/ppermute | solution.py:19
  269.0 16.0 %collective-permute-start.44 = (f32[96,768]{1,0:T(8,128)S(1)}, f32[96,768]{1,0:T(8,128)S(1)}, u32[]{:S(2)}, u32[]{:S(2)}) collective-permute-start(f32[96,768]{1,0:T(8,128)S(1)} %fusion.28), channel_id=1, source_target_pairs={{0,64},{32,96},{64,0},{96,32},{1,65},{33,97},{65,1},{97,33},{2,66}... | collective-permute-start | bytes 884744 | tf_op jit(solution)/shard_map/ppermute | solution.py:19
  271.3 15.8 %collective-permute-start.45 = (f32[96,768]{1,0:T(8,128)S(1)}, f32[96,768]{1,0:T(8,128)S(1)}, u32[]{:S(2)}, u32[]{:S(2)}) collective-permute-start(f32[96,768]{1,0:T(8,128)S(1)} %fusion.28), channel_id=1, source_target_pairs={{0,32},{32,64},{64,96},{96,0},{1,33},{33,65},{65,97},{97,1},{2,34}... | collective-permute-start | bytes 884744 | tf_op jit(solution)/shard_map/ppermute | solution.py:19
  304.9 22.5 %collective-permute-start.50 = (f32[768,768]{1,0:T(8,128)}, f32[768,768]{1,0:T(8,128)}, u32[]{:S(2)}, u32[]{:S(2)}) collective-permute-start(f32[768,768]{1,0:T(8,128)} %pad_maximum_fusion.1), channel_id=1, source_target_pairs={{0,4},{4,0},{1,5},{5,1},{2,6},{6,2},{3,7},{7,3},{8,12},{12,8},{9,1... | collective-permute-start | bytes 7077896 | tf_op jit(solution)/shard_map/ppermute | solution.py:19
  (34 other events, 268.4 us)

commit v2 on v0

v2 whole, which is shorter than its diff:
```python
import jax
import jax.numpy as jnp
from jax import lax
from jax.experimental import pallas as pl
from jax.experimental.pallas import tpu as pltpu
from jax.sharding import Mesh, PartitionSpec as P

F32 = jnp.float32
BF16 = jnp.bfloat16
STEPS = (2, 1, 3)


def shifted(value, axis, step):
    count = lax.axis_size(axis)
    return lax.ppermute(value, axis, [(i, (i + step) % count) for i in range(count)])


def crossed(value, tower, half):
    flip = 2 * half + tower
    return lax.ppermute(value, ("m", "t"), [(i, i ^ flip) for i in range(4)])


def pick(block, index, size, axis=0):
    return lax.dynamic_slice_in_dim(block, index * size, size, axis)


def tied(*values):
    return lax.optimization_barrier(values)


def tile_kernel(diag_ref, scale_ref, *refs):
    rows_refs, cols_refs = refs[:4], refs[4:12]
    ga_refs, gb_refs, la_ref, lb_ref = refs[12:16], refs[16:24], refs[24], refs[25]
    acc_ref, loss_ref = refs[26], refs[27]
    part, width = rows_refs[0].shape
    scale = scale_ref[0]
    bias = scale_ref[1]
    for step in range(4):
        gb = [jnp.zeros((part, width), F32) for _ in range(2)]
        for r in range(4):
            here = pl.ds(r * part, part)
            images = rows_refs[r][...]
            grad = jnp.zeros((part, width), F32)
            for core in range(2):
                texts = cols_refs[2 * step + core][...]
                logits = (
                    lax.dot_general(
                        images, texts, (((1,), (1,)), ((), ())), preferred_element_type=F32
                    )
                    * scale
                    + bias
                )
                if step == 0 and r == 0 and core == 0:
                    image = lax.broadcasted_iota(jnp.int32, (part, part), 0)
                    text = lax.broadcasted_iota(jnp.int32, (part, part), 1)
                    same = image + diag_ref[0] == text
                    logits = jnp.where(same, -logits, logits)
                grown = jnp.exp(logits)
                whole = 1.0 + grown
                inverse = 1.0 / whole
                losses = jnp.log(whole) + (grown - (whole - 1.0)) * inverse
                share = grown * inverse
                if step == 0 and r == 0 and core == 0:
                    share = jnp.where(same, -share, share)
                coefficient = share.astype(BF16)
                folded = sum(losses[:, k * 128 : (k + 1) * 128] for k in range(part // 128))
                column = jnp.sum(losses, axis=0, keepdims=True)
                if step == 0 and core == 0:
                    loss_ref[here, :] = folded
                else:
                    loss_ref[here, :] += folded
                if r == 0:
                    lb_ref[2 * step + core] = column
                else:
                    lb_ref[2 * step + core] += column
                grad += jnp.dot(coefficient, texts, preferred_element_type=F32)
                gb[core] += lax.dot_general(
                    coefficient, images, (((0,), (0,)), ((), ())), preferred_element_type=F32
                )
            if step == 0:
                acc_ref[here, :] = grad
            elif step < 3:
                acc_ref[here, :] += grad
            else:
                ga_refs[r][...] = (acc_ref[here, :] + grad).astype(BF16)
        for core in range(2):
            gb_refs[2 * step + core][...] = gb[core].astype(BF16)
    la_ref[...] = jnp.sum(loss_ref[...], axis=1, keepdims=True)


def tile_terms(rows, cols, diag, scales):
    part, width = rows[0].shape
    smem = pl.BlockSpec(memory_space=pltpu.SMEM)
    vmem = pl.BlockSpec(memory_space=pltpu.VMEM)
    piece = jax.ShapeDtypeStruct((part, width), BF16)
    out = pl.pallas_call(
        tile_kernel,
        in_specs=[smem, smem] + [vmem] * 12,
        out_specs=[vmem] * 14,
        out_shape=[piece] * 12
        + [
            jax.ShapeDtypeStruct((4 * part, 1), F32),
            jax.ShapeDtypeStruct((8, 1, part), F32),
        ],
        scratch_shapes=[
            pltpu.VMEM((4 * part, width), F32),
            pltpu.VMEM((4 * part, 128), F32),
        ],
        compiler_params=pltpu.CompilerParams(vmem_limit_bytes=56 * 2**20),
        cost_estimate=pl.CostEstimate(
            flops=6 * 4 * 8 * part * part * width,
            bytes_accessed=2 * 24 * part * width,
            transcendentals=3 * 32 * part * part,
        ),
    )(diag, scales, *rows, *cols)
    return out[:4], out[4:12], out[12], out[13]


def on_device(features, projection, similarity_scale, logit_bias):
    x, y, c = lax.axis_index("x"), lax.axis_index("y"), lax.axis_index("c")
    m, t = lax.axis_index("m"), lax.axis_index("t")
    inputs = features[0]
    rows, width = inputs.shape
    weight = projection[0]
    half = weight.shape[1]
    part = rows // 2
    pairs = rows * 32
    scale_factor = similarity_scale[0]

    projected = jnp.dot(inputs, weight, preferred_element_type=F32)
    squares = lax.psum(jnp.sum(projected * projected, axis=1), "m")[:, None]
    inverse = lax.rsqrt(squares + 1e-06)
    embedded = (projected * inverse).astype(BF16)
    mine = pick(inputs, c, half, 1)
    others = shifted(pick(inputs, 1 - c, half, 1), "c", 1)

    def rows_for(tower, flip):
        return pick(embedded, jnp.where(t == 0, m ^ flip, 1 ^ tower), part)

    kept = rows_for(0, 0)
    far, near, cross = tied(
        crossed(rows_for(1, 0), 1, 0), crossed(rows_for(0, 1), 0, 1), crossed(rows_for(1, 1), 1, 1)
    )
    own = jnp.concatenate([kept, near], axis=1)
    other = jnp.concatenate([far, cross], axis=1)
    own, other = tied(own, other)

    r2, c2, r1, c1, r3, c3 = tied(
        *(shifted(v, a, k) for k in STEPS for v, a in ((own, "y"), (other, "x")))
    )
    row_pieces = [own, r1, r2, r3]
    col_pieces = [other, c1, c2, c3]
    col_others = [shifted(piece, "c", 1) for piece in col_pieces]
    diag = jnp.where(m == t, 0, 2 * part).astype(jnp.int32).reshape(1)
    scales = jnp.stack([scale_factor, logit_bias[0]])
    cols = [piece for both in zip(col_pieces, col_others) for piece in both]
    grad_rows, grad_cols, loss_rows, loss_cols = tile_terms(row_pieces, cols, diag, scales)

    given = [shifted(grad_cols[2 * k + 1], "c", 1) for k in range(4)]
    sums = [(grad_cols[2 * k].astype(F32) + given[k].astype(F32)).astype(BF16) for k in range(4)]
    r2, c2, r1, c1, r3, c3 = tied(
        *(shifted(v[k], a, 4 - k) for k in STEPS for v, a in ((grad_rows, "y"), (sums, "x")))
    )
    grad_own = sum(v.astype(F32) for v in (grad_rows[0], r1, r2, r3)).astype(BF16)
    grad_other = sum(v.astype(F32) for v in (sums[0], c1, c2, c3)).astype(BF16)

    loss_rows = loss_rows.reshape(4, part)
    loss_rows = loss_rows[0] + sum(shifted(loss_rows[k], "y", 4 - k) for k in STEPS)
    loss_cols = loss_cols.reshape(4, 2, part)
    loss_cols = loss_cols[:, 0] + shifted(loss_cols[:, 1], "c", 1)
    loss_cols = loss_cols[0] + sum(shifted(loss_cols[k], "x", 4 - k) for k in STEPS)
    loss_far = crossed(loss_cols, 1, 0)
    loss_near = crossed(jnp.where(m == 0, loss_rows, loss_far), 0, 1)
    kept = jnp.where(jnp.logical_and(t == 1, m == 0), 0.0, loss_rows)
    row_loss = (kept + jnp.where(jnp.logical_and(t == 1, m == 1), 0.0, loss_far)) + jnp.where(
        t == 1, loss_near, 0.0
    )
    row_loss = row_loss / pairs

    far, near, cross = tied(
        crossed(grad_other[:, :half], 1, 0),
        crossed(grad_own[:, half:], 0, 1),
        crossed(grad_other[:, half:], 1, 1),
    )
    g00, g10, g01, g11 = (v.astype(F32) for v in (grad_own[:, :half], far, near, cross))
    first = jnp.where(t == 0, jnp.where(m == 0, g00 + g10, g01 + g11), g10 + g11)
    second = jnp.where(t == 0, jnp.where(m == 0, g01 + g11, g00 + g10), g00 + g01)
    grad_embed = jnp.concatenate([first, second], axis=0) * (scale_factor / pairs)
    grad_embed, row_loss = tied(grad_embed, row_loss)

    along = lax.psum(jnp.sum(projected * grad_embed, axis=1), "m")[:, None]
    cubed = inverse * inverse * inverse
    grad_proj = (inverse * grad_embed - cubed * projected * along).astype(BF16)
    grad_swap = shifted(grad_proj, "c", 1)
    weight_part = lax.dot_general(
        mine, grad_proj, (((0,), (0,)), ((), ())), preferred_element_type=F32
    ) + lax.dot_general(others, grad_swap, (((0,), (0,)), ((), ())), preferred_element_type=F32)

    quarter = half // 2
    small = quarter // 4
    one, two = weight_part[:quarter], weight_part[quarter:]
    a2, b2, a1, b1, a3, b3 = tied(
        *(
            shifted(pick(v, (p + k) % 4, small), a, k)
            for k in STEPS
            for v, p, a in ((one, x, "x"), (two, y, "y"))
        )
    )
    one = pick(one, x, small) + a1 + a2 + a3
    two = pick(two, y, small) + b1 + b2 + b3
    a2, b2, a1, b1, a3, b3 = tied(
        *(shifted(v, a, k) for k in STEPS for v, a in ((one, "y"), (two, "x")))
    )
    one = one + a1 + a2 + a3
    two = two + b1 + b2 + b3
    a2, b2, a1, b1, a3, b3 = tied(
        *(shifted(v, a, k) for k in STEPS for v, a in ((one, "x"), (two, "y")))
    )
    whole = jnp.zeros((half, half), F32)
    for k, (a, b) in enumerate(((one, two), (a1, b1), (a2, b2), (a3, b3))):
        whole = lax.dynamic_update_slice_in_dim(whole, a, (x - k) % 4 * small, 0)
        whole = lax.dynamic_update_slice_in_dim(whole, b, quarter + (y - k) % 4 * small, 0)
    swapped = shifted(whole, "c", 1)
    weight_grad = jnp.zeros((2, half, half), F32)
    weight_grad = lax.dynamic_update_index_in_dim(weight_grad, whole, c, 0)
    weight_grad = lax.dynamic_update_index_in_dim(weight_grad, swapped, 1 - c, 0)
    return (row_loss[None], weight_grad.reshape(1, width, half))


def solution(mesh):
    fine = Mesh(mesh.devices.reshape(4, 4, 2, 2, 2), ("x", "y", "c", "m", "t"))
    dp = ("x", "y", "c")
    placed = (P("t", dp, None), P("t", None, "m"), P(), P())
    return jax.shard_map(
        on_device,
        mesh=fine,
        in_specs=placed,
        out_specs=(P("t", dp + ("m",)), P("t", None, "m")),
        check_vma=False,
    )
```

time: 465 us -> 288 us (0.62)
  waiting for transfers between devices: 356 us -> 122 us
  starting transfers between devices: 2.7 us -> 75.5 us
  matrix products: 62.4 us -> 6.68 us
  Pallas kernels: 0 us -> 29.1 us
  other arithmetic: 6.12 us -> 19.1 us
  between operations: 15.1 us -> 2.51 us
  local copies, waits for them, and re-layouts: 9.44 us -> 19.8 us
    all_gather x2 -> x0, waiting for transfers between devices: 209 us -> none  [the longest x1 158 us: on_device(): rows_per_block = lax.all_gather(partner_block, 'dp', axis=0, tiled=True)]
    psum x1 -> x0, waiting for transfers between devices: 112 us -> none  [on_device(): weight_grad = lax.psum(weight_part, 'dp')]
    ppermute x1 -> x56, waiting for transfers between devices: 34.4 us -> 122 us  [the longest x48 97 us: shifted(): lax.ppermute(value, axis, [(i, (i + step) % count) for i in range(count)])]
    ppermute x1 -> x56, starting transfers between devices: 2.58 us -> 75.5 us  [the longest x48 63.8 us: shifted(): lax.ppermute(value, axis, [(i, (i + step) % count) for i in range(count)])]
    dot_general x4 -> x3, matrix products: 62.4 us -> 6.68 us  [the longest x1 3.93 us: on_device(): projected = jnp.dot(inputs, weight, preferred_element_type=F32)]
    pallas_call x0 -> x1, Pallas kernels: none -> 29.1 us  [tile_terms(): pl.pallas_call(tile_kernel, in_specs=[smem, smem] + [vmem] * 12, out_spec...]
    all_to_all x1 -> x0, blocking collectives: 12.8 us -> none  [on_device(): lax.all_to_all(grad_rows, 'mp', split_axis=1, concat_axis=0, tiled=True)]
    psum x0 -> x2, blocking collectives: none -> 8.54 us  [the longest x1 4.76 us: on_device(): squares = lax.psum(jnp.sum(projected * projected, axis=1), 'm')[:, None]]
  transfers between devices with their start and end apart: 4 -> 56, of which waited for: 4 -> 26; matrix products, arithmetic and copies ran while one was open for 0% -> 8% of each run, Pallas kernels for 0% -> 0%
where the time goes in v2:
time: 288 us; the launch traced here: 283 us
  waiting for transfers between devices  122 us (42%)
  starting transfers between devices  75.5 us (26%)
  Pallas kernels  29.1 us (10%)
  local copies, waits for them, and re-layouts  19.8 us (7%)
  other arithmetic  19.1 us (7%)
  blocking collectives  8.54 us (3%)
  matrix products  6.68 us (2%)
    ppermute x48, waiting for transfers between devices, shifted(): lax.ppermute(value, axis, [(i, (i + step) % count) for i in range(count)])  97 us
    ppermute x48, starting transfers between devices, shifted(): lax.ppermute(value, axis, [(i, (i + step) % count) for i in range(count)])  63.8 us
    pallas_call x1, Pallas kernels, tile_terms(): pl.pallas_call(tile_kernel, in_specs=[smem, smem] + [vmem] * 12, out_spec...  29.1 us
    ppermute x8, waiting for transfers between devices, crossed(): return lax.ppermute(value, ('m', 't'), [(i, i ^ flip) for i in range(4)])  24.7 us
    ppermute x8, starting transfers between devices, crossed(): return lax.ppermute(value, ('m', 't'), [(i, i ^ flip) for i in range(4)])  11.7 us
    unnamed x37, local copies, waits for them, and re-layouts  6.09 us
  transfers between devices with their start and end apart: 56, of which 26 were waited for; matrix products, arithmetic and copies ran while one was open for 8% of the time, Pallas kernels for 0%

profile of v2, /device:TPU:1, one launch (start us, length us, event | category | flops | bytes accessed | tf_op | source)
XLA Modules:
  0.0 283.0 jit_solution(16967537382423737935)
XLA Ops:
  2.3 3.9 %multiply_reduce_fusion.1 = (f32[512]{0:T(512)S(1)}, f32[512,768]{1,0:T(8,128)}) fusion(bf16[1,1536,768]{2,1,0:T(8,128)(2,1)S(1)} %copy-done, bf16[1,512,1536]{2,1,0:T(8,128)(2,1)} %param.4), kind=kOutput, calls=%fused_computation.16 | convolution fusion | flops 1208745472 | bytes 5507072 | tf_op jit(solution)/shard_map/dot_general | solution.py:130
  6.2 4.8 %psum.14 = f32[512]{0:T(512)S(1)} all-reduce(f32[512]{0:T(512)S(1)} %get-tuple-element.144), channel_id=1, replica_groups=mesh['x'=4,'y'=4,'c'=2,'m'=2,'t'=2] {'m'}, use_global_device_ids=true, to_apply=%region_1.0 | all-reduce | flops 512 | bytes 4096 | tf_op jit(solution)/shard_map/psum | solution.py:131
  12.7 3.5 %collective-permute-start = (bf16[256,768]{1,0:T(8,128)(2,1)S(1)}, bf16[256,768]{1,0:T(8,128)(2,1)S(1)}, u32[]{:S(2)}, u32[]{:S(2)}) collective-permute-start(bf16[256,768]{1,0:T(8,128)(2,1)S(1)} %get-tuple-element.135), channel_id=1, source_target_pairs={{0,1},{1,0},{2,3},{3,2},{4,5},{5,4},{6,7},{7,6},{8,9},{9,8},{10,11... | collective-permute-start | bytes 1179656 | tf_op jit(solution)/shard_map/ppermute | solution.py:20
  17.0 6.9 %collective-permute-done = bf16[256,768]{1,0:T(8,128)(2,1)S(1)} collective-permute-done((bf16[256,768]{1,0:T(8,128)(2,1)S(1)}, bf16[256,768]{1,0:T(8,128)(2,1)S(1)}, u32[]{:S(2)}, u32[]{:S(2)}) %collective-permute-start) | collective-permute-done | bytes 393248 | tf_op jit(solution)/shard_map/ppermute | solution.py:20
  23.9 8.9 %collective-permute-done.1 = bf16[256,768]{1,0:T(8,128)(2,1)S(1)} collective-permute-done((bf16[256,768]{1,0:T(8,128)(2,1)S(1)}, bf16[256,768]{1,0:T(8,128)(2,1)S(1)}, u32[]{:S(2)}, u32[]{:S(2)}) %collective-permute-start.1) | collective-permute-done | bytes 393248 | tf_op jit(solution)/shard_map/ppermute | solution.py:20
  43.1 10.8 %collective-permute-done.3.refs_2_ = bf16[256,1536]{1,0:T(8,128)(2,1)S(1)} collective-permute-done((bf16[256,1536]{1,0:T(8,128)(2,1)S(1)}, bf16[256,1536]{1,0:T(8,128)(2,1)S(1)}, u32[]{:S(2)}, u32[]{:S(2)}) %collective-permute-start.3) | collective-permute-done | bytes 786464 | tf_op jit(solution)/shard_map/ppermute | solution.py:15
  56.5 4.6 %collective-permute-start.9 = (bf16[256,1536]{1,0:T(8,128)(2,1)S(1)}, bf16[256,1536]{1,0:T(8,128)(2,1)}, u32[]{:S(2)}, u32[]{:S(2)}) collective-permute-start(bf16[256,1536]{1,0:T(8,128)(2,1)S(1)} %get-tuple-element.60.refs_4_), channel_id=1, source_target_pairs={{0,4},{4,0},{1,5},{5,1},{2,6},{6,2},{3,7},{7,3},{8,12},{12,8},{9,1... | collective-permute-start | bytes 2359304 | tf_op jit(solution)/shard_map/ppermute | solution.py:15
  61.0 11.3 %collective-permute-done.5.refs_1_ = bf16[256,1536]{1,0:T(8,128)(2,1)S(1)} collective-permute-done((bf16[256,1536]{1,0:T(8,128)(2,1)S(1)}, bf16[256,1536]{1,0:T(8,128)(2,1)S(1)}, u32[]{:S(2)}, u32[]{:S(2)}) %collective-permute-start.5) | collective-permute-done | bytes 786464 | tf_op jit(solution)/shard_map/ppermute | solution.py:15
  80.4 29.1 %shard_map.59 = (bf16[256,1536]{1,0:T(8,128)(2,1)}, bf16[256,1536]{1,0:T(8,128)(2,1)}, bf16[256,1536]{1,0:T(8,128)(2,1)}, bf16[256,1536]{1,0:T(8,128)(2,1)}, bf1...) custom-call(s32[1]{0:T(128)} %bitcast.diag_ref, ...), custom_call_target="tpu_custom_call" | custom-call | flops 19327352832 | bytes 18874368 | tf_op jit(solution)/shard_map/pallas_call | solution.py:96
  126.0 6.2 %collective-permute-done.13 = bf16[256,1536]{1,0:T(8,128)(2,1)} collective-permute-done((bf16[256,1536]{1,0:T(8,128)(2,1)}, bf16[256,1536]{1,0:T(8,128)(2,1)}, u32[]{:S(2)}, u32[]{:S(2)}) %collective-permute-start.13) | collective-permute-done | bytes 786464 | tf_op jit(solution)/shard_map/ppermute | solution.py:15
  135.7 11.8 %collective-permute-done.16 = bf16[256,1536]{1,0:T(8,128)(2,1)} collective-permute-done((bf16[256,1536]{1,0:T(8,128)(2,1)}, bf16[256,1536]{1,0:T(8,128)(2,1)}, u32[]{:S(2)}, u32[]{:S(2)}) %collective-permute-start.16) | collective-permute-done | bytes 786464 | tf_op jit(solution)/shard_map/ppermute | solution.py:15
  153.0 4.6 %collective-permute-done.15 = bf16[256,1536]{1,0:T(8,128)(2,1)S(1)} collective-permute-done((bf16[256,1536]{1,0:T(8,128)(2,1)}, bf16[256,1536]{1,0:T(8,128)(2,1)S(1)}, u32[]{:S(2)}, u32[]{:S(2)}) %collective-permute-start.15) | collective-permute-done | bytes 786464 | tf_op jit(solution)/shard_map/ppermute | solution.py:15
  157.7 3.4 %collective-permute-start.33 = (f32[256]{0:T(256)S(1)}, f32[256]{0:T(256)S(1)}, u32[]{:S(2)}, u32[]{:S(2)}) collective-permute-start(f32[256]{0:T(256)S(1)} %add_add_fusion.4), channel_id=1, source_target_pairs={{0,1},{1,0},{2,3},{3,2},{4,5},{5,4},{6,7},{7,6},{8,9},{9,8},{10,11... | collective-permute-start | bytes 3080 | tf_op jit(solution)/shard_map/ppermute | solution.py:20
  170.8 6.1 %collective-permute-start.35 = (bf16[512,768]{1,0:T(8,128)(2,1)}, bf16[512,768]{1,0:T(8,128)(2,1)S(1)}, u32[]{:S(2)}, u32[]{:S(2)}) collective-permute-start(bf16[512,768]{1,0:T(8,128)(2,1)} %dynamic-slice_bitcast_fusion), channel_id=1, source_target_pairs={{0,4},{4,0},{1,5},{5,1},{2,6},{6,2},{3,7},{7,3},{8,12},{12,8},{9,1... | collective-permute-start | bytes 2359304 | tf_op jit(solution)/shard_map/ppermute | solution.py:15
  178.1 6.8 %collective-permute-done.25 = bf16[256,768]{1,0:T(8,128)(2,1)S(1)} collective-permute-done((bf16[256,768]{1,0:T(8,128)(2,1)S(1)}, bf16[256,768]{1,0:T(8,128)(2,1)S(1)}, u32[]{:S(2)}, u32[]{:S(2)}) %collective-permute-start.25) | collective-permute-done | bytes 393248 | tf_op jit(solution)/shard_map/ppermute | solution.py:20
  188.4 3.8 %psum.15 = f32[512]{0:T(512)S(1)} all-reduce(f32[512]{0:T(512)S(1)} %multiply_reduce_fusion), channel_id=1, replica_groups=mesh['x'=4,'y'=4,'c'=2,'m'=2,'t'=2] {'m'}, use_global_device_ids=true, to_apply=%region_3.4 | all-reduce | flops 512 | bytes 4096 | tf_op jit(solution)/shard_map/psum | solution.py:191
  193.9 4.2 %collective-permute-start.36 = (bf16[512,768]{1,0:T(8,128)(2,1)S(1)}, bf16[512,768]{1,0:T(8,128)(2,1)S(1)}, u32[]{:S(2)}, u32[]{:S(2)}) collective-permute-start(bf16[512,768]{1,0:T(8,128)(2,1)S(1)} %subtract_convert_fusion), channel_id=1, source_target_pairs={{0,4},{4,0},{1,5},{5,1},{2,6},{6,2},{3,7},{7,3},{8,12},{12,8},{9,1... | collective-permute-start | bytes 2359304 | tf_op jit(solution)/shard_map/ppermute | solution.py:15
  213.0 5.1 %collective-permute-done.40 = f32[96,768]{1,0:T(8,128)} collective-permute-done((f32[96,768]{1,0:T(8,128)S(1)}, f32[96,768]{1,0:T(8,128)}, u32[]{:S(2)}, u32[]{:S(2)}) %collective-permute-start.40) | collective-permute-done | bytes 294944 | tf_op jit(solution)/shard_map/ppermute | solution.py:15
  218.1 4.7 %collective-permute-done.39 = f32[96,768]{1,0:T(8,128)} collective-permute-done((f32[96,768]{1,0:T(8,128)}, f32[96,768]{1,0:T(8,128)}, u32[]{:S(2)}, u32[]{:S(2)}) %collective-permute-start.39) | collective-permute-done | bytes 294944 | tf_op jit(solution)/shard_map/ppermute | solution.py:15
  234.5 6.4 %collective-permute-done.46 = f32[96,768]{1,0:T(8,128)S(1)} collective-permute-done((f32[96,768]{1,0:T(8,128)S(1)}, f32[96,768]{1,0:T(8,128)S(1)}, u32[]{:S(2)}, u32[]{:S(2)}) %collective-permute-start.46) | collective-permute-done | bytes 294944 | tf_op jit(solution)/shard_map/ppermute | solution.py:15
  240.9 5.2 %collective-permute-done.45 = f32[96,768]{1,0:T(8,128)S(1)} collective-permute-done((f32[96,768]{1,0:T(8,128)S(1)}, f32[96,768]{1,0:T(8,128)S(1)}, u32[]{:S(2)}, u32[]{:S(2)}) %collective-permute-start.45) | collective-permute-done | bytes 294944 | tf_op jit(solution)/shard_map/ppermute | solution.py:15
  253.4 5.5 %collective-permute-done.50 = f32[96,768]{1,0:T(8,128)S(1)} collective-permute-done((f32[96,768]{1,0:T(8,128)S(1)}, f32[96,768]{1,0:T(8,128)S(1)}, u32[]{:S(2)}, u32[]{:S(2)}) %collective-permute-start.50) | collective-permute-done | bytes 294944 | tf_op jit(solution)/shard_map/ppermute | solution.py:15
  258.9 7.1 %collective-permute-done.52 = f32[96,768]{1,0:T(8,128)S(1)} collective-permute-done((f32[96,768]{1,0:T(8,128)S(1)}, f32[96,768]{1,0:T(8,128)S(1)}, u32[]{:S(2)}, u32[]{:S(2)}) %collective-permute-start.52) | collective-permute-done | bytes 294944 | tf_op jit(solution)/shard_map/ppermute | solution.py:15
  266.0 3.4 %collective-permute-done.51 = f32[96,768]{1,0:T(8,128)S(1)} collective-permute-done((f32[96,768]{1,0:T(8,128)S(1)}, f32[96,768]{1,0:T(8,128)S(1)}, u32[]{:S(2)}, u32[]{:S(2)}) %collective-permute-start.51) | collective-permute-done | bytes 294944 | tf_op jit(solution)/shard_map/ppermute | solution.py:15
  (174 shorter events, 112.4 us)
Async XLA Ops:
  16.2 16.6 %collective-permute-start.1 = (bf16[256,768]{1,0:T(8,128)(2,1)S(1)}, bf16[256,768]{1,0:T(8,128)(2,1)S(1)}, u32[]{:S(2)}, u32[]{:S(2)}) collective-permute-start(bf16[256,768]{1,0:T(8,128)(2,1)S(1)} %get-tuple-element.134), channel_id=1, source_target_pairs={{0,2},{1,3},{2,0},{3,1},{4,6},{5,7},{6,4},{7,5},{8,10},{9,11},{10,... | collective-permute-start | bytes 1179656 | tf_op jit(solution)/shard_map/ppermute | solution.py:20
  17.0 17.3 %collective-permute-start.2 = (bf16[256,768]{1,0:T(8,128)(2,1)S(1)}, bf16[256,768]{1,0:T(8,128)(2,1)S(1)}, u32[]{:S(2)}, u32[]{:S(2)}) collective-permute-start(bf16[256,768]{1,0:T(8,128)(2,1)S(1)} %get-tuple-element.133), channel_id=1, source_target_pairs={{0,3},{1,2},{2,1},{3,0},{4,7},{5,6},{6,5},{7,4},{8,11},{9,10},{10,... | collective-permute-start | bytes 1179656 | tf_op jit(solution)/shard_map/ppermute | solution.py:20
  34.4 19.5 %collective-permute-start.3 = (bf16[256,1536]{1,0:T(8,128)(2,1)S(1)}, bf16[256,1536]{1,0:T(8,128)(2,1)S(1)}, u32[]{:S(2)}, u32[]{:S(2)}) collective-permute-start(bf16[256,1536]{1,0:T(8,128)(2,1)S(1)} %get-tuple-element.59.refs_0_), channel_id=1, source_target_pairs={{0,16},{8,24},{16,0},{24,8},{1,17},{9,25},{17,1},{25,9},{2,18},{10... | collective-permute-start | bytes 2359304 | tf_op jit(solution)/shard_map/ppermute | solution.py:15
  37.3 19.1 %collective-permute-start.4 = (bf16[256,1536]{1,0:T(8,128)(2,1)S(1)}, bf16[256,1536]{1,0:T(8,128)(2,1)}, u32[]{:S(2)}, u32[]{:S(2)}) collective-permute-start(bf16[256,1536]{1,0:T(8,128)(2,1)S(1)} %get-tuple-element.60.refs_4_), channel_id=1, source_target_pairs={{0,64},{32,96},{64,0},{96,32},{1,65},{33,97},{65,1},{97,33},{2,66}... | collective-permute-start | bytes 2359304 | tf_op jit(solution)/shard_map/ppermute | solution.py:15
  40.1 32.3 %collective-permute-start.5 = (bf16[256,1536]{1,0:T(8,128)(2,1)S(1)}, bf16[256,1536]{1,0:T(8,128)(2,1)S(1)}, u32[]{:S(2)}, u32[]{:S(2)}) collective-permute-start(bf16[256,1536]{1,0:T(8,128)(2,1)S(1)} %get-tuple-element.59.refs_0_), channel_id=1, source_target_pairs={{0,8},{8,16},{16,24},{24,0},{1,9},{9,17},{17,25},{25,1},{2,10},{10... | collective-permute-start | bytes 2359304 | tf_op jit(solution)/shard_map/ppermute | solution.py:15
  40.5 34.8 %collective-permute-start.6 = (bf16[256,1536]{1,0:T(8,128)(2,1)S(1)}, bf16[256,1536]{1,0:T(8,128)(2,1)}, u32[]{:S(2)}, u32[]{:S(2)}) collective-permute-start(bf16[256,1536]{1,0:T(8,128)(2,1)S(1)} %get-tuple-element.60.refs_4_), channel_id=1, source_target_pairs={{0,32},{32,64},{64,96},{96,0},{1,33},{33,65},{65,97},{97,1},{2,34}... | collective-permute-start | bytes 2359304 | tf_op jit(solution)/shard_map/ppermute | solution.py:15
  40.8 34.5 %collective-permute-start.7 = (bf16[256,1536]{1,0:T(8,128)(2,1)S(1)}, bf16[256,1536]{1,0:T(8,128)(2,1)S(1)}, u32[]{:S(2)}, u32[]{:S(2)}) collective-permute-start(bf16[256,1536]{1,0:T(8,128)(2,1)S(1)} %get-tuple-element.59.refs_0_), channel_id=1, source_target_pairs={{0,24},{8,0},{16,8},{24,16},{1,25},{9,1},{17,9},{25,17},{2,26},{10... | collective-permute-start | bytes 2359304 | tf_op jit(solution)/shard_map/ppermute | solution.py:15
  53.8 21.4 %collective-permute-start.8 = (bf16[256,1536]{1,0:T(8,128)(2,1)S(1)}, bf16[256,1536]{1,0:T(8,128)(2,1)}, u32[]{:S(2)}, u32[]{:S(2)}) collective-permute-start(bf16[256,1536]{1,0:T(8,128)(2,1)S(1)} %get-tuple-element.60.refs_4_), channel_id=1, source_target_pairs={{0,96},{32,0},{64,32},{96,64},{1,97},{33,1},{65,33},{97,65},{2,98}... | collective-permute-start | bytes 2359304 | tf_op jit(solution)/shard_map/ppermute | solution.py:15
  56.5 22.3 %collective-permute-start.9 = (bf16[256,1536]{1,0:T(8,128)(2,1)S(1)}, bf16[256,1536]{1,0:T(8,128)(2,1)}, u32[]{:S(2)}, u32[]{:S(2)}) collective-permute-start(bf16[256,1536]{1,0:T(8,128)(2,1)S(1)} %get-tuple-element.60.refs_4_), channel_id=1, source_target_pairs={{0,4},{4,0},{1,5},{5,1},{2,6},{6,2},{3,7},{7,3},{8,12},{12,8},{9,1... | collective-permute-start | bytes 2359304 | tf_op jit(solution)/shard_map/ppermute | solution.py:15
  111.5 20.6 %collective-permute-start.13 = (bf16[256,1536]{1,0:T(8,128)(2,1)}, bf16[256,1536]{1,0:T(8,128)(2,1)}, u32[]{:S(2)}, u32[]{:S(2)}) collective-permute-start(bf16[256,1536]{1,0:T(8,128)(2,1)} %get-tuple-element.68), channel_id=1, source_target_pairs={{0,16},{8,24},{16,0},{24,8},{1,17},{9,25},{17,1},{25,9},{2,18},{10... | collective-permute-start | bytes 2359304 | tf_op jit(solution)/shard_map/ppermute | solution.py:15
  119.8 27.7 %collective-permute-start.16 = (bf16[256,1536]{1,0:T(8,128)(2,1)}, bf16[256,1536]{1,0:T(8,128)(2,1)}, u32[]{:S(2)}, u32[]{:S(2)}) collective-permute-start(bf16[256,1536]{1,0:T(8,128)(2,1)} %get-tuple-element.71), channel_id=1, source_target_pairs={{0,24},{8,0},{16,8},{24,16},{1,25},{9,1},{17,9},{25,17},{2,26},{10... | collective-permute-start | bytes 2359304 | tf_op jit(solution)/shard_map/ppermute | solution.py:15
  121.1 28.6 %collective-permute-start.19 = (bf16[256,1536]{1,0:T(8,128)(2,1)}, bf16[256,1536]{1,0:T(8,128)(2,1)}, u32[]{:S(2)}, u32[]{:S(2)}) collective-permute-start(bf16[256,1536]{1,0:T(8,128)(2,1)} %get-tuple-element.74), channel_id=1, source_target_pairs={{0,8},{8,16},{16,24},{24,0},{1,9},{9,17},{17,25},{25,1},{2,10},{10... | collective-permute-start | bytes 2359304 | tf_op jit(solution)/shard_map/ppermute | solution.py:15
  122.2 29.1 %collective-permute-start.21 = (bf16[256,1536]{1,0:T(8,128)(2,1)S(1)}, bf16[256,1536]{1,0:T(8,128)(2,1)S(1)}, u32[]{:S(2)}, u32[]{:S(2)}) collective-permute-start(bf16[256,1536]{1,0:T(8,128)(2,1)S(1)} %add_convert_fusion.3), channel_id=1, source_target_pairs={{0,32},{32,64},{64,96},{96,0},{1,33},{33,65},{65,97},{97,1},{2,34}... | collective-permute-start | bytes 2359304 | tf_op jit(solution)/shard_map/ppermute | solution.py:15
  122.7 30.3 %collective-permute-start.18 = (bf16[256,1536]{1,0:T(8,128)(2,1)}, bf16[256,1536]{1,0:T(8,128)(2,1)S(1)}, u32[]{:S(2)}, u32[]{:S(2)}) collective-permute-start(bf16[256,1536]{1,0:T(8,128)(2,1)} %add_convert_fusion.4), channel_id=1, source_target_pairs={{0,96},{32,0},{64,32},{96,64},{1,97},{33,1},{65,33},{97,65},{2,98}... | collective-permute-start | bytes 2359304 | tf_op jit(solution)/shard_map/ppermute | solution.py:15
  132.1 25.5 %collective-permute-start.15 = (bf16[256,1536]{1,0:T(8,128)(2,1)}, bf16[256,1536]{1,0:T(8,128)(2,1)S(1)}, u32[]{:S(2)}, u32[]{:S(2)}) collective-permute-start(bf16[256,1536]{1,0:T(8,128)(2,1)} %add_convert_fusion.5), channel_id=1, source_target_pairs={{0,64},{32,96},{64,0},{96,32},{1,65},{33,97},{65,1},{97,33},{2,66}... | collective-permute-start | bytes 2359304 | tf_op jit(solution)/shard_map/ppermute | solution.py:15
  149.7 16.4 %collective-permute-start.26 = (f32[256]{0:T(256)S(1)}, f32[256]{0:T(256)S(1)}, u32[]{:S(2)}, u32[]{:S(2)}) collective-permute-start(f32[256]{0:T(256)S(1)} %get-tuple-element.112), channel_id=1, source_target_pairs={{0,16},{8,24},{16,0},{24,8},{1,17},{9,25},{17,1},{25,9},{2,18},{10... | collective-permute-start | bytes 3080 | tf_op jit(solution)/shard_map/ppermute | solution.py:15
  153.0 16.2 %collective-permute-start.28 = (f32[256]{0:T(256)S(1)}, f32[256]{0:T(256)S(1)}, u32[]{:S(2)}, u32[]{:S(2)}) collective-permute-start(f32[256]{0:T(256)S(1)} %get-tuple-element.111), channel_id=1, source_target_pairs={{0,8},{8,16},{16,24},{24,0},{1,9},{9,17},{17,25},{25,1},{2,10},{10... | collective-permute-start | bytes 3080 | tf_op jit(solution)/shard_map/ppermute | solution.py:15
  166.9 18.0 %collective-permute-start.25 = (bf16[256,768]{1,0:T(8,128)(2,1)S(1)}, bf16[256,768]{1,0:T(8,128)(2,1)S(1)}, u32[]{:S(2)}, u32[]{:S(2)}) collective-permute-start(bf16[256,768]{1,0:T(8,128)(2,1)S(1)} %get-tuple-element.130), channel_id=1, source_target_pairs={{0,3},{1,2},{2,1},{3,0},{4,7},{5,6},{6,5},{7,4},{8,11},{9,10},{10,... | collective-permute-start | bytes 1179656 | tf_op jit(solution)/shard_map/ppermute | solution.py:20
  170.8 29.3 %collective-permute-start.35 = (bf16[512,768]{1,0:T(8,128)(2,1)}, bf16[512,768]{1,0:T(8,128)(2,1)S(1)}, u32[]{:S(2)}, u32[]{:S(2)}) collective-permute-start(bf16[512,768]{1,0:T(8,128)(2,1)} %dynamic-slice_bitcast_fusion), channel_id=1, source_target_pairs={{0,4},{4,0},{1,5},{5,1},{2,6},{6,2},{3,7},{7,3},{8,12},{12,8},{9,1... | collective-permute-start | bytes 2359304 | tf_op jit(solution)/shard_map/ppermute | solution.py:15
  202.1 16.0 %collective-permute-start.40 = (f32[96,768]{1,0:T(8,128)S(1)}, f32[96,768]{1,0:T(8,128)}, u32[]{:S(2)}, u32[]{:S(2)}) collective-permute-start(f32[96,768]{1,0:T(8,128)S(1)} %get-tuple-element.125), channel_id=1, source_target_pairs={{0,8},{8,16},{16,24},{24,0},{1,9},{9,17},{17,25},{25,1},{2,10},{10... | collective-permute-start | bytes 884744 | tf_op jit(solution)/shard_map/ppermute | solution.py:15
  230.1 16.1 %collective-permute-start.45 = (f32[96,768]{1,0:T(8,128)S(1)}, f32[96,768]{1,0:T(8,128)S(1)}, u32[]{:S(2)}, u32[]{:S(2)}) collective-permute-start(f32[96,768]{1,0:T(8,128)S(1)} %add_add_fusion.3), channel_id=1, source_target_pairs={{0,8},{8,16},{16,24},{24,0},{1,9},{9,17},{17,25},{25,1},{2,10},{10... | collective-permute-start | bytes 884744 | tf_op jit(solution)/shard_map/ppermute | solution.py:15
  249.9 16.1 %collective-permute-start.52 = (f32[96,768]{1,0:T(8,128)S(1)}, f32[96,768]{1,0:T(8,128)S(1)}, u32[]{:S(2)}, u32[]{:S(2)}) collective-permute-start(f32[96,768]{1,0:T(8,128)S(1)} %get-tuple-element.115), channel_id=1, source_target_pairs={{0,8},{8,16},{16,24},{24,0},{1,9},{9,17},{17,25},{25,1},{2,10},{10... | collective-permute-start | bytes 884744 | tf_op jit(solution)/shard_map/ppermute | solution.py:15
  249.9 16.1 %collective-permute-start.54 = (f32[96,768]{1,0:T(8,128)S(1)}, f32[96,768]{1,0:T(8,128)S(1)}, u32[]{:S(2)}, u32[]{:S(2)}) collective-permute-start(f32[96,768]{1,0:T(8,128)S(1)} %get-tuple-element.115), channel_id=1, source_target_pairs={{0,24},{8,0},{16,8},{24,16},{1,25},{9,1},{17,9},{25,17},{2,26},{10... | collective-permute-start | bytes 884744 | tf_op jit(solution)/shard_map/ppermute | solution.py:15
  253.3 16.1 %collective-permute-start.51 = (f32[96,768]{1,0:T(8,128)S(1)}, f32[96,768]{1,0:T(8,128)S(1)}, u32[]{:S(2)}, u32[]{:S(2)}) collective-permute-start(f32[96,768]{1,0:T(8,128)S(1)} %get-tuple-element.117), channel_id=1, source_target_pairs={{0,32},{32,64},{64,96},{96,0},{1,33},{33,65},{65,97},{97,1},{2,34}... | collective-permute-start | bytes 884744 | tf_op jit(solution)/shard_map/ppermute | solution.py:15
  (50 other events, 497.1 us)
